TPU v7x, 32 devices: a whole 2x2x4 slice. The times are simulated.
32 devices in a mesh: groups: 2 (over y), adapters: 4 (over z), tp: 2 (over x), sub: 2 (over core).
Axes of the slice: x: 2, y: 2, z: 4, core: 2. Of those that a mesh axis runs over, the one named last changes fastest.
Arguments:
- tokens: bfloat16 [16384, 8192], P(('groups', 'adapters', 'sub'), 'tp'), parts along dimension 0, may hold values from -6 to 6
- token_adapter_index: int32 [16384, 1], P(('groups', 'adapters', 'sub')), parts along dimension 0, may hold values from 0 to 31; in each aligned block of 1024 rows (0 to 1023, 1024 to 2047, ...) at most 64 rows name the same one
- adapter_slot_table: int32 [32], replicated, may hold values from 0 to 31, each once
- base_value_matrix: bfloat16 [8192, 1024], P(None, 'tp'), may hold values from -0.0625 to 0.0625
- adapter_down_weight: bfloat16 [32, 8192, 64], P(('adapters', 'sub'), 'tp'), may hold values from -0.0625 to 0.0625
- adapter_up_weight: bfloat16 [32, 64, 1024], P(('adapters', 'sub'), None, 'tp'), may hold values from -0.75 to 0.75
- adapter_scale_rows: float32 [32], P(('adapters', 'sub')), may hold values from 0.5 to 2
Outputs:
- values: bfloat16 [16384, 1024], P(('groups', 'adapters', 'sub'), 'tp'), parts along dimension 0
There are 2 independent parts, one for each index of `groups`. A program takes and returns all parts, laid end to end along the dimension named above; an argument that names none is the same for every part. Nothing has to cross between parts.
Inputs may be any that keep to these rules, and one draw needn't show every extreme that they name: `token_adapter_index`: in each aligned block of 1024 rows (the rows of one index of adapters and sub) no adapter is named by more than 64 rows, a bound that some block reaches; every adapter is named somewhere. `adapter_slot_table`: A permutation: every stored row is used by exactly one adapter.
All inputs are finite; a program needn't handle non-finite values.
Results may differ from a plain program's by a relative error of at most 0.0051.
Values may be sent and summed in bfloat16 or wider, within the bound.
A program may use at most 192 MiB of HBM per device.

v0:
```python
import jax
import jax.numpy as jnp
from jax import lax
from jax.sharding import PartitionSpec as P


def holder_workload(arrived_rows, adapter_down_weight, adapter_up_weight, adapter_scale_rows):
    partial_rank = jnp.einsum(
        "umwk,mkn->umwn", arrived_rows, adapter_down_weight, preferred_element_type=jnp.float32
    )
    rank_product = lax.psum(partial_rank, "tp").astype(jnp.bfloat16)
    lowrank_delta_rows = jnp.einsum(
        "znye,neg->znyg", rank_product, adapter_up_weight, preferred_element_type=jnp.float32
    )
    return (lowrank_delta_rows * adapter_scale_rows[None, :, None, None]).astype(jnp.bfloat16)


def local(
    tokens,
    token_adapter_index,
    adapter_slot_table,
    base_value_matrix,
    adapter_down_weight,
    adapter_up_weight,
    adapter_scale_rows,
):
    row_count = tokens.shape[0]
    feat_count = tokens.shape[1]
    adapter_count = adapter_slot_table.shape[0]
    resident_count = adapter_down_weight.shape[0]
    owner_count = adapter_count // resident_count
    capacity = 2 * row_count // adapter_count
    out_count = base_value_matrix.shape[1]
    base_sum = jnp.dot(
        lax.all_gather(tokens, "tp", axis=1, tiled=True),
        base_value_matrix,
        preferred_element_type=jnp.float32,
    )
    slot_iota = jnp.arange(adapter_count, dtype=jnp.int32)
    is_named = (token_adapter_index == slot_iota[None, :]).astype(jnp.int32)
    stored_slot = jnp.sum(is_named * adapter_slot_table[None, :], axis=1)
    stored = (stored_slot[:, None] == slot_iota[None, :]).astype(jnp.int32)
    before = jnp.cumsum(stored, axis=0) - stored
    slot_rank = jnp.sum(before * stored, axis=1)
    send_row = stored_slot * capacity + slot_rank
    outgoing = (
        jnp.zeros((adapter_count * capacity, feat_count), tokens.dtype).at[send_row].set(tokens)
    )
    outgoing = outgoing.reshape(owner_count, resident_count, capacity, feat_count)
    lowrank_delta_rows = holder_workload(
        lax.all_to_all(outgoing, ("adapters", "sub"), split_axis=0, concat_axis=0, tiled=True),
        adapter_down_weight,
        adapter_up_weight,
        adapter_scale_rows,
    )
    returned = lax.all_to_all(
        lowrank_delta_rows, ("adapters", "sub"), split_axis=0, concat_axis=0, tiled=True
    )
    flat_delta = returned.reshape(adapter_count * capacity, out_count)
    own_delta = flat_delta[send_row]
    return (base_sum + own_delta.astype(jnp.float32)).astype(jnp.bfloat16)


def solution(mesh):
    in_specs = (
        P(("groups", "adapters", "sub"), "tp"),
        P(("groups", "adapters", "sub"), None),
        P(),
        P(None, "tp"),
        P(("adapters", "sub"), "tp", None),
        P(("adapters", "sub"), None, "tp"),
        P(("adapters", "sub")),
    )
    out_specs = P(("groups", "adapters", "sub"), "tp")
    return jax.shard_map(local, mesh=mesh, in_specs=in_specs, out_specs=out_specs, check_vma=False)
```

profile of v0, /device:TPU:0, one launch (start us, length us, event | category | flops | bytes accessed | tf_op | source)
XLA Modules:
  0.0 529.6 jit_solution(9833083902379735408)
XLA Ops:
  6.5 0.0 copy-start
  6.5 0.9 select_reduce_fusion
  7.5 9.0 %reduce-window.6 = s32[32,8,128]{2,1,0:T(8,128)S(1)} reduce-window(s32[32,8,128]{2,1,0:T(8,128)S(1)} %fusion.16, s32[]{:T(128)} %constant.5.clone.1), window={size=1x1x128 pad=0_0x0_0x127_0}, to_apply=%region_1.0 | reduce-window | flops 4161536 | bytes 262148 | tf_op jit(solution)/shard_map/reduce-window
  16.5 0.1 slice.10
  16.6 0.1 copy.18
  16.8 0.1 copy.19
  16.9 0.1 broadcast_add_fusion
  17.0 22.0 %scatter_custom_fusion = bf16[2048,4096]{1,0:T(8,128)(2,1)} fusion(s32[1024]{0:T(1024)S(1)} %bitcast.49, bf16[1024,4096]{1,0:T(8,128)(2,1)} %param.7, bf16[]{:T(256)} %constant.4.clone.1), kind=kCustom, calls=%fused_computation.4 | custom fusion | bytes 16777728 | tf_op jit(solution)/shard_map/scatter | solution.py:47
  39.0 6.3 %all-to-all-start = ((bf16[8,4,64,4096]{3,2,1,0:T(8,128)(2,1)}), bf16[8,4,64,4096]{3,2,1,0:T(8,128)(2,1)}, u32[]{:S(2)}, u32[]{:S(2)}) async-start(bf16[8,4,64,4096]{3,2,1,0:T(8,128)(2,1)} %bitcast.43), calls=%async_computation | async-start | bytes 33554432 | tf_op jit(solution)/shard_map/all_to_all | solution.py:51
  45.3 0.0 all-gather.2.cloned.1.call-start
  45.4 0.7 all-gather.2.cloned.1.call-update
  46.1 0.0 copy-start.2
  46.1 0.0 copy-start.3
  46.1 363.1 %all-to-all-done = bf16[8,4,64,4096]{3,2,1,0:T(8,128)(2,1)} async-done(((bf16[8,4,64,4096]{3,2,1,0:T(8,128)(2,1)}), bf16[8,4,64,4096]{3,2,1,0:T(8,128)(2,1)}, u32[]{:S(2)}, u32[]{:S(2)}) %all-to-all-start) | async-done | bytes 16777248 | tf_op jit(solution)/shard_map/all_to_all | solution.py:51
  409.2 0.0 copy-done
  409.2 9.1 %fusion.6 = f32[8,4,64,64]{3,2,0,1:T(8,128)} fusion(bf16[4,4096,64]{1,2,0:T(8,128)(2,1)S(1)} %copy-done, bf16[8,4,64,4096]{3,2,1,0:T(8,128)(2,1)} %all-to-all-done), kind=kOutput, calls=%fused_computation.10 | convolution fusion | flops 1073741824 | bytes 19398656 | tf_op jit(solution)/shard_map/umwk,mkn->umwn/dot_general | solution.py:8
  418.2 30.0 %all-reduce.1 = bf16[8,4,64,64]{3,2,0,1:T(8,128)(2,1)S(1)} all-reduce(f32[8,4,64,64]{3,2,0,1:T(8,128)} %fusion.6), channel_id=1, replica_groups=mesh['groups'=2,'adapters'=4,'tp'=2,'sub'=2] {'tp'}, use_global_device_ids=true, to_apply=%region_5.6 | all-reduce | flops 131072 | bytes 786432 | tf_op jit(solution)/shard_map/psum | solution.py:11
  448.2 0.0 copy-done.2
  448.2 0.0 copy-done.3
  448.2 0.7 fusion.5
  448.9 1.6 copy.21
  450.5 3.6 all-to-all-start.1
  454.1 49.0 %all-to-all-done.1 = bf16[8,4,64,512]{3,2,1,0:T(8,128)(2,1)S(1)} async-done(((bf16[8,4,64,512]{3,2,1,0:T(8,128)(2,1)}), bf16[8,4,64,512]{3,2,1,0:T(8,128)(2,1)S(1)}, u32[]{:S(2)}, u32[]{:S(2)}) %all-to-all-start.1) | async-done | bytes 2097184 | tf_op jit(solution)/shard_map/all_to_all | solution.py:56
  503.1 4.0 gather_fusion
  507.0 0.0 all-gather.2.cloned.1.call-done
  507.1 0.0 copy-start.1
  507.1 15.7 %add_convert_fusion = bf16[1024,512]{1,0:T(8,128)(2,1)} fusion(bf16[1024,512]{1,0:T(8,128)(2,1)S(1)} %gather_fusion, bf16[1024,8192]{1,0:T(8,128)(2,1)} %all-gather.2.cloned.1.call-done, bf16[8192,512]{1,0:T(8,128)(2,1)} %param.10), kind=kOutput, calls=%fused_computation.8 | convolution fusion | flops 8591507456 | bytes 27262976 | tf_op jit(solution)/shard_map/dot_general | solution.py:34
  522.8 0.0 copy-done.1
  (7 shorter events, 0.1 us)
Async XLA Ops:
  6.5 402.6 %copy-start = (bf16[4,4096,64]{1,2,0:T(8,128)(2,1)S(1)}, bf16[4,4096,64]{1,2,0:T(8,128)(2,1)}, u32[]{:S(2)}) copy-start(bf16[4,4096,64]{1,2,0:T(8,128)(2,1)} %param.11) | copy-start | bytes 6291460
  39.0 370.2 %all-to-all-start = ((bf16[8,4,64,4096]{3,2,1,0:T(8,128)(2,1)}), bf16[8,4,64,4096]{3,2,1,0:T(8,128)(2,1)}, u32[]{:S(2)}, u32[]{:S(2)}) async-start(bf16[8,4,64,4096]{3,2,1,0:T(8,128)(2,1)} %bitcast.43), calls=%async_computation | async-start | bytes 33554432 | tf_op jit(solution)/shard_map/all_to_all | solution.py:51
  45.3 461.7 %all-gather.2.cloned.1.call-start = ((), (), s32[]{:S(2)}) async-start(), calls=%async_computation.2 | async-start | bytes 25165824 | tf_op jit(solution)/shard_map/all_gather | solution.py:35
  46.1 402.1 %copy-start.2 = (bf16[4,64,512]{2,1,0:T(8,128)(2,1)S(1)}, bf16[4,64,512]{2,1,0:T(8,128)(2,1)}, u32[]{:S(2)}) copy-start(bf16[4,64,512]{2,1,0:T(8,128)(2,1)} %param.12) | copy-start | bytes 786436
  46.1 402.1 %copy-start.3 = (f32[4]{0:T(128)S(1)}, f32[4]{0:T(128)}, u32[]{:S(2)}) copy-start(f32[4]{0:T(128)} %param.13) | copy-start | bytes 52
  450.5 52.6 %all-to-all-start.1 = ((bf16[8,4,64,512]{3,2,1,0:T(8,128)(2,1)}), bf16[8,4,64,512]{3,2,1,0:T(8,128)(2,1)S(1)}, u32[]{:S(2)}, u32[]{:S(2)}) async-start(bf16[8,4,64,512]{3,2,1,0:T(8,128)(2,1)} %copy.21), calls=%async_computation.1 | async-start | bytes 4194304 | tf_op jit(solution)/shard_map/all_to_all | solution.py:56
  507.1 15.7 %copy-start.1 = (bf16[4,4096,64]{1,2,0:T(8,128)(2,1)S(1)}, bf16[4,4096,64]{1,2,0:T(8,128)(2,1)}, u32[]{:S(2)}) copy-start(bf16[4,4096,64]{1,2,0:T(8,128)(2,1)} %param.11) | copy-start | bytes 6291460
Sparse Core Ops, SparseCore 0:
  47.7 201.0 all-gather.1
where the time goes:
time: 530 us
  waiting for transfers between devices  413 us (78%)
  blocking collectives  30 us (6%)
  local copies, waits for them, and re-layouts  27.8 us (5%)
  matrix products  25.4 us (5%)
  between operations  13.5 us (3%)
  other arithmetic  10.2 us (2%)
  starting transfers between devices  9.96 us (2%)
    all_to_all x1, waiting for transfers between devices, local(): lax.all_to_all(outgoing, ('adapters', 'sub'), split_axis=0, concat_axis=0...  363 us
    all_to_all x1, waiting for transfers between devices, local(): lax.all_to_all(lowrank_delta_rows, ('adapters', 'sub'), split_axis=0, con...  49 us
    psum x1, blocking collectives, holder_workload(): rank_product = lax.psum(partial_rank, 'tp').astype(jnp.bfloat16)  30 us
    scatter x1, local copies, waits for them, and re-layouts, local(): jnp.zeros((adapter_count * capacity, feat_count), tokens.dtype).at[send_row]  22 us
    dot_general x1, matrix products, local(): jnp.dot(lax.all_gather(tokens, 'tp', axis=1, tiled=True), base_value_matr...  15.7 us
  transfers between devices with their start and end apart: 3, of which 2 were waited for; matrix products, arithmetic and copies ran while one was open for 3% of the time, Pallas kernels for 0%

commit v1 on v0

v1 whole, which is shorter than its diff:
```python
import functools

import jax
import jax.numpy as jnp
from jax import lax
from jax.experimental import pallas as pl
from jax.experimental.pallas import tpu as pltpu
from jax.sharding import PartitionSpec as P

LANES = 128
PARTS = 4


def kernel(
    depth,
    tok_hbm, base_hbm, down_hbm, up_hbm, key_ref,
    out_ref,
    tok, wmine, wcross, buf, acc, pout, pin, lacc, sacc, lpo, lpi,
    local_sem, send_z, recv_z, send_y, recv_y, send_c, recv_c, send_x, recv_x,
):
    rows, feats = tok.shape
    held_rows = buf.shape[1]
    outs = wmine.shape[1]
    half_outs = outs // 2
    half_feats = feats // 2
    half = held_rows // 2
    step_rows = half // PARTS
    tile = min(512, rows)
    g = lax.axis_index("groups")
    z = lax.axis_index("adapters")
    p = lax.axis_index("tp")
    s = lax.axis_index("sub")
    me = 2 * z + s

    def remote(src, dst, send, recv, to):
        return pltpu.make_async_remote_copy(
            src_ref=src, dst_ref=dst, send_sem=send, recv_sem=recv,
            device_id=to, device_id_type=pl.DeviceIdType.MESH,
        )

    def piece(owner, h, q):
        start = pl.multiple_of(h * half + q * step_rows, step_rows)
        return buf.at[owner, pl.ds(start, step_rows)]

    def source(d, k):
        return z - k if d == 0 else z + k

    def exists(d, k):
        return z >= k if d == 0 else z + k < depth

    def can_send(d):
        return z + 1 < depth if d == 0 else z >= 1

    x_to, y_to, c_to = {"tp": 1 - p}, {"groups": 1 - g}, {"sub": 1 - s}

    def z_copy(d, k, q):
        block = piece(2 * source(d, k) + s, g, q)
        to = {"adapters": z + 1 if d == 0 else z - 1}
        return remote(block, block, send_z.at[d, k, q], recv_z.at[d, k, q], to)

    def z_arrival(d, k, q):
        block = piece(2 * source(d, k + 1) + s, g, q)
        return remote(block, block, send_z.at[d, k, q], recv_z.at[d, k, q], x_to)

    def y_copy(d, k, q, h):
        block = piece(2 * source(d, k + 1) + s, h, q)
        return remote(block, block, send_y.at[d, k, q], recv_y.at[d, k, q], y_to)

    def c_copy(d, k, q, w, core):
        block = piece(2 * source(d, k + 1) + core, g if w == 0 else 1 - g, q)
        return remote(block, block, send_c.at[d, k, q, w], recv_c.at[d, k, q, w], c_to)

    def own_copy(core):
        block = buf.at[2 * z + core]
        return remote(block, block, send_x.at[0], recv_x.at[0], c_to)

    def x_copy(c):
        first = pl.multiple_of((1 - p) * feats + s * half_feats, half_feats)
        return remote(
            base_hbm.at[pl.ds(first, half_feats), pl.ds(c * half_outs, half_outs)],
            wcross.at[c, pl.ds(pl.multiple_of(s * half_feats, half_feats), half_feats)],
            send_x.at[1 + c], recv_x.at[1 + c], x_to,
        )

    def xc_copy(c, core):
        block = wcross.at[c, pl.ds(pl.multiple_of(core * half_feats, half_feats), half_feats)]
        return remote(block, block, send_x.at[3 + c], recv_x.at[3 + c], c_to)

    def part_copy(c):
        return remote(pout.at[c], pin.at[c], send_x.at[5 + c], recv_x.at[5 + c], x_to)

    def low_copy():
        return remote(lpo, lpi, send_x.at[7], recv_x.at[7], x_to)

    loads = [
        pltpu.make_async_copy(down_hbm, buf.at[me, :, pl.ds(0, feats)], local_sem.at[0]),
        pltpu.make_async_copy(up_hbm, buf.at[me, :, pl.ds(feats, outs + LANES)], local_sem.at[1]),
        pltpu.make_async_copy(tok_hbm, tok, local_sem.at[2]),
        pltpu.make_async_copy(
            base_hbm.at[pl.ds(pl.multiple_of(p * feats, feats), feats)], wmine, local_sem.at[3]
        ),
    ]
    for load in loads:
        load.start()

    barrier = pltpu.get_barrier_semaphore()
    for to in (x_to, y_to, c_to):
        pl.semaphore_signal(barrier, inc=1, device_id=to, device_id_type=pl.DeviceIdType.MESH)
    for d in range(2):
        @pl.when(can_send(d))
        def _(d=d):
            to = {"adapters": z + 1 if d == 0 else z - 1}
            pl.semaphore_signal(barrier, inc=1, device_id=to, device_id_type=pl.DeviceIdType.MESH)
    pl.semaphore_wait(barrier, 3 + (z >= 1).astype(jnp.int32) + (z + 1 < depth).astype(jnp.int32))

    for c in range(2):
        x_copy(c).start()
    loads[0].wait()
    loads[1].wait()
    for q in range(PARTS):
        for d in range(2):
            @pl.when(can_send(d))
            def _(d=d, q=q):
                z_copy(d, 0, q).start()
    own_copy(s).start()

    def project(owner):
        @pl.loop(0, rows // tile)
        def _(i):
            at = pl.ds(pl.multiple_of(i * tile, tile), tile)
            wide = lax.dot_general(
                tok[at], buf[owner, :, pl.ds(0, feats)], (((1,), (1,)), ((), ())),
                preferred_element_type=jnp.float32,
            )
            key = key_ref[at]
            first, second = key == 4 * owner, key == 4 * owner + 2
            lacc[at] += jnp.where(first, wide[:, :LANES], 0.0) + jnp.where(second, wide[:, LANES:], 0.0)
            ones = jnp.concatenate(
                [jnp.where(first, 1.0, 0.0), jnp.where(second, 1.0, 0.0)], axis=1
            ).astype(jnp.bfloat16)
            sacc[at] += jnp.dot(
                ones, buf[owner, :, pl.ds(feats + outs, LANES)], preferred_element_type=jnp.float32
            )

    def z_events(k, q):
        for d in range(2):
            @pl.when(exists(d, k + 1))
            def _(d=d):
                z_arrival(d, k, q).wait_recv()
                if k + 1 < depth - 1:
                    @pl.when(can_send(d))
                    def _():
                        z_copy(d, k + 1, q).start()
                y_copy(d, k, q, g).start()
                c_copy(d, k, q, 0, s).start()

    def y_events(k, q):
        for d in range(2):
            @pl.when(exists(d, k + 1))
            def _(d=d):
                y_copy(d, k, q, 1 - g).wait_recv()
                c_copy(d, k, q, 1, s).start()

    def owners(d, k):
        @pl.when(exists(d, k + 1))
        def _():
            for q in range(PARTS):
                for w in range(2):
                    c_copy(d, k, q, w, 1 - s).wait_recv()

            @pl.loop(0, 2)
            def _(core):
                project(2 * source(d, k + 1) + core)

    def take_cross(c):
        x_copy_in = remote(
            wcross.at[c, pl.ds(pl.multiple_of(s * half_feats, half_feats), half_feats)],
            wcross.at[c, pl.ds(pl.multiple_of(s * half_feats, half_feats), half_feats)],
            send_x.at[1 + c], recv_x.at[1 + c], x_to,
        )
        x_copy_in.wait_recv()
        xc_copy(c, s).start()

    def cross(c):
        xc_copy(c, 1 - s).wait_recv()

        @pl.loop(0, rows // tile)
        def _(i):
            at = pl.ds(pl.multiple_of(i * tile, tile), tile)
            pout[c, at] = jnp.dot(
                tok[at], wcross[c], preferred_element_type=jnp.float32
            ).astype(jnp.bfloat16)

        part_copy(c).start()

    lacc[...] = jnp.zeros_like(lacc)
    sacc[...] = jnp.zeros_like(sacc)
    loads[2].wait()
    project(me)
    loads[3].wait()

    @pl.loop(0, rows // tile)
    def _(i):
        at = pl.ds(pl.multiple_of(i * tile, tile), tile)
        for c in range(2):
            cols = pl.ds(c * half_outs, half_outs)
            acc[at, cols] = jnp.dot(tok[at], wmine[:, cols], preferred_element_type=jnp.float32)

    def sibling():
        own_copy(1 - s).wait_recv()
        project(2 * z + 1 - s)

    steps = (depth - 1) * PARTS
    tasks = {1: [sibling], 3: [lambda: take_cross(0)], 4: [lambda: cross(0)],
             7: [lambda: take_cross(1)], 8: [lambda: cross(1)]}
    for k in range(depth - 1):
        tasks.setdefault(k * PARTS + PARTS + 1, []).append(lambda k=k: owners(0, k))
        tasks.setdefault(k * PARTS + PARTS + 2, []).append(lambda k=k: owners(1, k))
    for i in range(max(steps, max(tasks)) + 1):
        if i < steps:
            z_events(i // PARTS, i % PARTS)
        if 0 < i <= steps:
            y_events((i - 1) // PARTS, (i - 1) % PARTS)
        for task in tasks.get(i, []):
            task()

    folded = lacc[...] + pltpu.roll(lacc[...], LANES // 2, 1)
    low_lane = lax.broadcasted_iota(jnp.int32, lpo.shape, 1) < LANES // 2
    lpo[...] = jnp.where(low_lane, folded[: rows // 2], folded[rows // 2 :])
    low_copy().start()
    for c in range(2):
        part_copy(c).wait_recv()
    low_copy().wait_recv()
    both = lpo[...] + lpi[...]
    turned = pltpu.roll(both, LANES // 2, 1)
    lacc[pl.ds(0, rows // 2)] = jnp.where(low_lane, both, turned)
    lacc[pl.ds(rows // 2, rows // 2)] = jnp.where(low_lane, turned, both)

    end_tile = min(256, rows)

    @pl.loop(0, rows // end_tile)
    def _(i):
        at = pl.ds(pl.multiple_of(i * end_tile, end_tile), end_tile)
        low = lacc[at].astype(jnp.bfloat16).astype(jnp.float32)
        key = key_ref[at]
        spread = jnp.concatenate(
            [jnp.where(key == 2 * j, low, 0.0).astype(jnp.bfloat16) for j in range(4 * depth)], axis=1
        )
        scale = sacc[at]
        for c in range(2):
            cols = pl.ds(c * half_outs, half_outs)
            ups = buf[:, :, pl.ds(feats + c * half_outs, half_outs)].reshape(-1, half_outs)
            delta = jnp.dot(spread, ups, preferred_element_type=jnp.float32)
            wide_scale = jnp.concatenate([scale] * (half_outs // LANES), axis=1)
            delta = (delta * wide_scale).astype(jnp.bfloat16).astype(jnp.float32)
            base = acc[at, cols] + pin[c, at].astype(jnp.float32)
            out_ref[at, cols] = (base + delta).astype(jnp.bfloat16)

    for c in range(2):
        x_copy(c).wait_send()
        xc_copy(c, s).wait_send()
        part_copy(c).wait_send()
    low_copy().wait_send()
    own_copy(s).wait_send()
    for k in range(depth - 1):
        for d in range(2):
            @pl.when(exists(d, k) & can_send(d))
            def _(d=d, k=k):
                for q in range(PARTS):
                    z_copy(d, k, q).wait_send()

            @pl.when(exists(d, k + 1))
            def _(d=d, k=k):
                for q in range(PARTS):
                    y_copy(d, k, q, g).wait_send()
                    for w in range(2):
                        c_copy(d, k, q, w, s).wait_send()


def fused(depth, tokens, stored, base, down_rows, up_rows, scale_rows):
    rows, feats = tokens.shape
    held_rows, outs = up_rows.shape
    rank = held_rows // scale_rows.shape[0]
    high = lax.reduce_precision(scale_rows, 8, 7)
    mid = lax.reduce_precision(scale_rows - high, 8, 7)
    rest = scale_rows - high - mid
    place = jnp.arange(rank)[None, :]
    split = jnp.where(
        place == 0, high[:, None],
        jnp.where(place == 1, mid[:, None], jnp.where(place == 2, rest[:, None], 0.0)),
    )
    scale_cols = jnp.broadcast_to(split.reshape(held_rows, 1), (held_rows, LANES)).astype(jnp.bfloat16)
    up_wide = jnp.concatenate([up_rows, scale_cols], axis=1)
    lane = jnp.arange(LANES, dtype=jnp.int32)[None, :]
    key = stored[:, None] - (lane >= rank).astype(jnp.int32)
    bf16, f32 = jnp.bfloat16, jnp.float32
    hops = (2, depth - 1, PARTS)
    any_spec = pl.BlockSpec(memory_space=pl.ANY)
    vmem = pl.BlockSpec(memory_space=pltpu.VMEM)
    return pl.pallas_call(
        functools.partial(kernel, depth),
        out_shape=jax.ShapeDtypeStruct((rows, outs), bf16),
        in_specs=[any_spec] * 4 + [vmem],
        out_specs=vmem,
        scratch_shapes=[
            pltpu.VMEM((rows, feats), bf16),
            pltpu.VMEM((feats, outs), bf16),
            pltpu.VMEM((2, feats, outs // 2), bf16),
            pltpu.VMEM((2 * depth, held_rows, feats + outs + LANES), bf16),
            pltpu.VMEM((rows, outs), f32),
            pltpu.VMEM((2, rows, outs // 2), bf16),
            pltpu.VMEM((2, rows, outs // 2), bf16),
            pltpu.VMEM((rows, LANES), f32),
            pltpu.VMEM((rows, LANES), f32),
            pltpu.VMEM((rows // 2, LANES), f32),
            pltpu.VMEM((rows // 2, LANES), f32),
            pltpu.SemaphoreType.DMA((4,)),
            pltpu.SemaphoreType.DMA(hops),
            pltpu.SemaphoreType.DMA(hops),
            pltpu.SemaphoreType.DMA(hops),
            pltpu.SemaphoreType.DMA(hops),
            pltpu.SemaphoreType.DMA(hops + (2,)),
            pltpu.SemaphoreType.DMA(hops + (2,)),
            pltpu.SemaphoreType.DMA((8,)),
            pltpu.SemaphoreType.DMA((8,)),
        ],
        compiler_params=pltpu.CompilerParams(
            collective_id=0, has_side_effects=True, vmem_limit_bytes=58 * 1024 * 1024
        ),
    )(tokens, base, down_rows, up_wide, key)


def plain(tokens, stored, base, down_rows, up_rows, scale_rows, adapters):
    rows = tokens.shape[0]
    rank = down_rows.shape[0] // scale_rows.shape[0]
    owners = ("adapters", "sub")
    down_all = lax.all_gather(down_rows, owners, axis=0, tiled=True)
    up_all = lax.all_gather(up_rows, owners, axis=0, tiled=True)
    scale_all = lax.all_gather(scale_rows, owners, axis=0, tiled=True)
    base_rows = lax.all_to_all(base, "tp", split_axis=0, concat_axis=1, tiled=True)
    base_sum = lax.psum_scatter(
        jnp.dot(tokens, base_rows, preferred_element_type=jnp.float32),
        "tp", scatter_dimension=1, tiled=True,
    )
    one_hot = stored[:, None] == jnp.arange(adapters, dtype=jnp.int32)[None, :]
    wide = lax.dot_general(
        tokens, down_all, (((1,), (1,)), ((), ())), preferred_element_type=jnp.float32
    )
    low = jnp.sum(jnp.where(one_hot[:, :, None], wide.reshape(rows, adapters, rank), 0.0), axis=1)
    low = lax.psum(low, "tp").astype(jnp.bfloat16)
    spread = jnp.where(one_hot[:, :, None], low[:, None, :], 0).reshape(rows, adapters * rank)
    delta = jnp.dot(spread, up_all, preferred_element_type=jnp.float32)
    scale = jnp.sum(jnp.where(one_hot, scale_all[None, :], 0.0), axis=1)
    delta = (delta * scale[:, None]).astype(jnp.bfloat16)
    return (base_sum + delta.astype(jnp.float32)).astype(jnp.bfloat16)


def local(
    sizes, tokens, token_adapter_index, adapter_slot_table, base, down, up, scale_rows
):
    held, feats, rank = down.shape
    adapters = adapter_slot_table.shape[0]
    outs = base.shape[1]
    slots = jnp.arange(adapters, dtype=jnp.int32)
    named = token_adapter_index == slots[None, :]
    stored = jnp.sum(jnp.where(named, adapter_slot_table[None, :], 0), axis=1)
    down_rows = jnp.swapaxes(down, 1, 2).reshape(held * rank, feats)
    up_rows = up.reshape(held * rank, outs)
    depth = sizes["adapters"]
    small = sizes["groups"] == sizes["tp"] == sizes["sub"] == 2 and 2 <= depth <= 4
    if small and held == 4 and 2 * rank == LANES:
        return fused(depth, tokens, stored, base, down_rows, up_rows, scale_rows)
    return plain(tokens, stored, base, down_rows, up_rows, scale_rows, adapters)


def solution(mesh):
    in_specs = (
        P(("groups", "adapters", "sub"), "tp"),
        P(("groups", "adapters", "sub"), None),
        P(),
        P(None, "tp"),
        P(("adapters", "sub"), "tp", None),
        P(("adapters", "sub"), None, "tp"),
        P(("adapters", "sub")),
    )
    out_specs = P(("groups", "adapters", "sub"), "tp")
    return jax.shard_map(
        functools.partial(local, dict(mesh.shape)), mesh=mesh,
        in_specs=in_specs, out_specs=out_specs, check_vma=False,
    )
```

time: 530 us -> 128 us (0.24)
  waiting for transfers between devices: 413 us -> 0 us
  Pallas kernels: 0 us -> 121 us
  blocking collectives: 30 us -> 0 us
  matrix products: 25.4 us -> 0 us
  local copies, waits for them, and re-layouts: 27.8 us -> 2.45 us
  between operations: 13.5 us -> 0.02 us
  starting transfers between devices: 9.96 us -> 0 us
  other arithmetic: 10.2 us -> 4.26 us
    all_to_all x2 -> x0, waiting for transfers between devices: 412 us -> none  [the longest x1 363 us: local(): lax.all_to_all(outgoing, ('adapters', 'sub'), split_axis=0, concat_axis=0...]
    pallas_call x0 -> x1, Pallas kernels: none -> 121 us  [fused(): pl.pallas_call(functools.partial(kernel, depth), out_shape=jax.ShapeDtype...]
    psum x1 -> x0, blocking collectives: 30 us -> none  [holder_workload(): rank_product = lax.psum(partial_rank, 'tp').astype(jnp.bfloat16)]
    dot_general x3 -> x0, matrix products: 25.4 us -> none  [the longest x1 15.7 us: local(): jnp.dot(lax.all_gather(tokens, 'tp', axis=1, tiled=True), base_value_matr...]
    scatter x1 -> x0, local copies, waits for them, and re-layouts: 22 us -> none  [local(): jnp.zeros((adapter_count * capacity, feat_count), tokens.dtype).at[send_row]]
    all_to_all x2 -> x0, starting transfers between devices: 9.93 us -> none  [the longest x1 6.33 us: local(): lax.all_to_all(outgoing, ('adapters', 'sub'), split_axis=0, concat_axis=0...]
    another operation x3 -> x0, other arithmetic: 9.15 us -> none
  transfers between devices with their start and end apart: 3 -> 0, of which waited for: 2 -> 0; matrix products, arithmetic and copies ran while one was open for 3% -> 0% of each run, Pallas kernels for 0% -> 0%
where the time goes in v1:
time: 128 us; the launch traced here: 127 us
  Pallas kernels  121 us (95%)
  other arithmetic  4.26 us (3%)
  local copies, waits for them, and re-layouts  2.45 us (2%)
    pallas_call x1, Pallas kernels, fused(): pl.pallas_call(functools.partial(kernel, depth), out_shape=jax.ShapeDtype...  121 us

profile of v1, /device:TPU:0, one launch (start us, length us, event | category | flops | bytes accessed | tf_op | source)
XLA Modules:
  0.0 127.4 jit_solution(2721563571993774663)
XLA Ops:
  0.0 0.7 fusion
  0.7 0.1 select_convert_fusion
  0.8 0.1 convert_element_type.16
  0.8 0.8 select_reduce_fusion
  1.6 0.1 broadcast_in_dim.78
  1.7 1.7 %pad_maximum_fusion.up_hbm = bf16[256,640]{1,0:T(8,128)(2,1)} fusion(bf16[256,128]{1,0:T(8,128)(2,1)S(1)} %broadcast_in_dim.78, bf16[256,512]{1,0:T(8,128)(2,1)} %bitcast.6), kind=kLoop, calls=%fused_computation | loop fusion | flops 655360 | bytes 655360 | tf_op jit(solution)/shard_map/concatenate | solution.py:293
  3.5 1.0 broadcast_subtract_fusion.key_ref
  4.5 120.7 %shard_map.73 = bf16[1024,512]{1,0:T(8,128)(2,1)} custom-call(bf16[1024,4096]{1,0:T(8,128)(2,1)} %tok_hbm.1, bf16[8192,512]{1,0:T(8,128)(2,1)} %base_hbm.1, bf16[256,4096]{1,0:T(8,128)(2,1)} %bitcast.5, bf16[256,640]{1,0:T(8,128)(2,1)} %pad_maximum_fusion.up_hbm, s32[1024,128]{1,0:T(8,128)} %broadcast_subtract_fusion.key_ref), custom_call_target="tpu_custom_call" | custom-call | tf_op jit(solution)/shard_map/pallas_call | solution.py:300
  125.2 2.3 %copy.9 = bf16[1024,512]{1,0:T(8,128)(2,1)} copy(bf16[1024,512]{1,0:T(8,128)(2,1)} %shard_map.73) | data formatting | bytes 2097152
  (3 shorter events, 0.0 us)

commit v2 on v1

v2 whole, which is shorter than its diff:
```python
import functools

import jax
import jax.numpy as jnp
from jax import lax
from jax.experimental import pallas as pl
from jax.experimental.pallas import tpu as pltpu
from jax.sharding import PartitionSpec as P

LANES = 128
PARTS = 4


def kernel(
    depth,
    tok_hbm, base_hbm, down_hbm, up_hbm, named_ref, table_ref, scale_ref,
    out_ref,
    tok, wmine, wcross, buf, ups, scales, key_ref, acc, pout, pin, lacc, lpo, lpi,
    local_sem, send_z, recv_z, send_y, recv_y, send_c, recv_c, send_x, recv_x,
):
    rows, feats = tok.shape
    held_rows = buf.shape[1]
    outs = wmine.shape[1]
    half_outs = outs // 2
    half_feats = feats // 2
    half = held_rows // 2
    step_rows = half // PARTS
    tile = rows // 2
    spots = tile // 2
    ups_part, scale_part = PARTS, PARTS + 1
    g = lax.axis_index("groups")
    z = lax.axis_index("adapters")
    p = lax.axis_index("tp")
    s = lax.axis_index("sub")
    me = 2 * z + s

    def remote(src, dst, send, recv, to):
        return pltpu.make_async_remote_copy(
            src_ref=src, dst_ref=dst, send_sem=send, recv_sem=recv,
            device_id=to, device_id_type=pl.DeviceIdType.MESH,
        )

    def piece(owner, h, q):
        if q == scale_part:
            return scales.at[owner]
        if q == ups_part:
            return ups.at[owner, pl.ds(pl.multiple_of(h * half, half), half)]
        start = pl.multiple_of(h * half + q * step_rows, step_rows)
        return buf.at[owner, pl.ds(start, step_rows)]

    def source(d, k):
        return z - k if d == 0 else z + k

    def exists(d, k):
        return z >= k if d == 0 else z + k < depth

    def can_send(d):
        return z + 1 < depth if d == 0 else z >= 1

    x_to, y_to, c_to = {"tp": 1 - p}, {"groups": 1 - g}, {"sub": 1 - s}

    def z_copy(d, k, q):
        block = piece(2 * source(d, k) + s, g, q)
        to = {"adapters": z + 1 if d == 0 else z - 1}
        first = block
        if k == 0 and q < PARTS:
            first = down_hbm.at[pl.ds(pl.multiple_of(g * half + q * step_rows, step_rows), step_rows)]
        elif k == 0 and q == ups_part:
            first = up_hbm.at[pl.ds(pl.multiple_of(g * half, half), half)]
        return remote(first, block, send_z.at[d, k, q], recv_z.at[d, k, q], to)

    def z_arrival(d, k, q):
        block = piece(2 * source(d, k + 1) + s, g, q)
        return remote(block, block, send_z.at[d, k, q], recv_z.at[d, k, q], x_to)

    def y_copy(d, k, q, h):
        block = piece(2 * source(d, k + 1) + s, h, q)
        return remote(block, block, send_y.at[d, k, q], recv_y.at[d, k, q], y_to)

    def c_copy(d, k, q, w, core):
        block = piece(2 * source(d, k + 1) + core, g if w == 0 else 1 - g, q)
        return remote(block, block, send_c.at[d, k, q, w], recv_c.at[d, k, q, w], c_to)

    def own_copies(core):
        owner = 2 * z + core
        return [
            remote(down_hbm, buf.at[owner], send_x.at[0], recv_x.at[0], c_to),
            remote(up_hbm, ups.at[owner], send_x.at[9], recv_x.at[9], c_to),
            remote(scales.at[owner], scales.at[owner], send_x.at[10], recv_x.at[10], c_to),
        ]

    def x_copy(c):
        first = pl.multiple_of((1 - p) * feats + s * half_feats, half_feats)
        return remote(
            base_hbm.at[pl.ds(first, half_feats), pl.ds(c * half_outs, half_outs)],
            wcross.at[c, pl.ds(pl.multiple_of(s * half_feats, half_feats), half_feats)],
            send_x.at[1 + c], recv_x.at[1 + c], x_to,
        )

    def xc_copy(c, core):
        block = wcross.at[c, pl.ds(pl.multiple_of(core * half_feats, half_feats), half_feats)]
        return remote(block, block, send_x.at[3 + c], recv_x.at[3 + c], c_to)

    def part_copy(c):
        return remote(pout.at[c], pin.at[c], send_x.at[5 + c], recv_x.at[5 + c], x_to)

    def low_copy(b):
        return remote(lpo.at[b], lpi.at[b], send_x.at[7 + b], recv_x.at[7 + b], x_to)

    loads = [
        pltpu.make_async_copy(down_hbm, buf.at[me], local_sem.at[0]),
        pltpu.make_async_copy(up_hbm, ups.at[me], local_sem.at[1]),
        pltpu.make_async_copy(tok_hbm, tok, local_sem.at[2]),
        pltpu.make_async_copy(
            base_hbm.at[pl.ds(pl.multiple_of(p * feats, feats), feats)], wmine, local_sem.at[3]
        ),
    ]
    for load in loads:
        load.start()

    lane = lax.broadcasted_iota(jnp.int32, (1, LANES), 1)
    for h in range(2):
        scales[me, pl.ds(h, 1)] = jnp.where(lane < LANES // 2, scale_ref[2 * h], scale_ref[2 * h + 1])

    barrier = pltpu.get_barrier_semaphore()
    for to in (x_to, y_to, c_to):
        pl.semaphore_signal(barrier, inc=1, device_id=to, device_id_type=pl.DeviceIdType.MESH)
    for d in range(2):
        @pl.when(can_send(d))
        def _(d=d):
            to = {"adapters": z + 1 if d == 0 else z - 1}
            pl.semaphore_signal(barrier, inc=1, device_id=to, device_id_type=pl.DeviceIdType.MESH)
    pl.semaphore_wait(barrier, 3 + (z >= 1).astype(jnp.int32) + (z + 1 < depth).astype(jnp.int32))

    for c in range(2):
        x_copy(c).start()
    for q in (*range(PARTS), ups_part, scale_part):
        for d in range(2):
            @pl.when(can_send(d))
            def _(d=d, q=q):
                z_copy(d, 0, q).start()
    for copy in own_copies(s):
        copy.start()

    def project_tile(owner, i):
        at = pl.ds(pl.multiple_of(i * tile, tile), tile)
        wide = lax.dot_general(
            tok[at], buf[owner], (((1,), (1,)), ((), ())), preferred_element_type=jnp.float32
        )
        key = key_ref[at]
        lacc[at] += jnp.where(key == 4 * owner, wide[:, :LANES], 0.0) + jnp.where(
            key == 4 * owner + 2, wide[:, LANES:], 0.0
        )

    def project(owner):
        @pl.loop(0, 2)
        def _(i):
            project_tile(owner, i)

    def z_events(k, q):
        for d in range(2):
            @pl.when(exists(d, k + 1))
            def _(d=d):
                z_arrival(d, k, q).wait_recv()
                if k + 1 < depth - 1:
                    @pl.when(can_send(d))
                    def _():
                        z_copy(d, k + 1, q).start()
                if q != scale_part:
                    y_copy(d, k, q, g).start()
                c_copy(d, k, q, 0, s).start()

    def y_events(k, q):
        for d in range(2):
            @pl.when(exists(d, k + 1))
            def _(d=d):
                y_copy(d, k, q, 1 - g).wait_recv()
                c_copy(d, k, q, 1, s).start()

    def arrived(d, k, parts):
        @pl.when(exists(d, k + 1))
        def _():
            for q in parts:
                for w in range(1 if q == scale_part else 2):
                    c_copy(d, k, q, w, 1 - s).wait_recv()

    def owners(d, k):
        arrived(d, k, range(PARTS))

        @pl.when(exists(d, k + 1))
        def _():
            @pl.loop(0, 2)
            def _(core):
                project(2 * source(d, k + 1) + core)

    def take_cross(c):
        x_copy_in = remote(
            wcross.at[c, pl.ds(pl.multiple_of(s * half_feats, half_feats), half_feats)],
            wcross.at[c, pl.ds(pl.multiple_of(s * half_feats, half_feats), half_feats)],
            send_x.at[1 + c], recv_x.at[1 + c], x_to,
        )
        x_copy_in.wait_recv()
        xc_copy(c, s).start()

    def cross(c):
        xc_copy(c, 1 - s).wait_recv()

        @pl.loop(0, rows // tile)
        def _(i):
            at = pl.ds(pl.multiple_of(i * tile, tile), tile)
            pout[c, at] = jnp.dot(
                tok[at], wcross[c], preferred_element_type=jnp.float32
            ).astype(jnp.bfloat16)

        part_copy(c).start()

    named = named_ref[...]
    stored = jnp.zeros_like(named)
    for a in range(table_ref.shape[0]):
        stored += jnp.where(named == a, table_ref[a], 0)
    stored = stored.astype(jnp.float32)
    for n in range(rows // LANES):
        square = jnp.broadcast_to(stored[n : n + 1], (LANES, LANES)).T.astype(jnp.int32)
        key_ref[pl.ds(n * LANES, LANES)] = square - (lane >= LANES // 2).astype(jnp.int32)
    lacc[...] = jnp.zeros_like(lacc)
    for load in loads[:3]:
        load.wait()
    project(me)
    loads[3].wait()

    @pl.loop(0, rows // tile)
    def _(i):
        at = pl.ds(pl.multiple_of(i * tile, tile), tile)
        for c in range(2):
            cols = pl.ds(c * half_outs, half_outs)
            acc[at, cols] = jnp.dot(tok[at], wmine[:, cols], preferred_element_type=jnp.float32)

    def sibling():
        own_copies(1 - s)[0].wait_recv()
        project(2 * z + 1 - s)

    steps = (depth - 1) * PARTS
    tasks = {1: [sibling], 3: [lambda: take_cross(0)], 4: [lambda: cross(0)],
             7: [lambda: take_cross(1)], 8: [lambda: cross(1)]}
    last = depth - 2
    for k in range(last):
        tasks.setdefault(k * PARTS + PARTS + 1, []).append(lambda k=k: owners(0, k))
        tasks.setdefault(k * PARTS + PARTS + 2, []).append(lambda k=k: owners(1, k))
    for i in range(max(steps, max(tasks)) + 1):
        if i < steps:
            z_events(i // PARTS, i % PARTS)
        if 0 < i <= steps:
            y_events((i - 1) // PARTS, (i - 1) % PARTS)
        for task in tasks.get(i, []):
            task()

    for k in range(last):
        for q in (ups_part, scale_part):
            z_events(k, q)
    for d in range(2):
        arrived(d, last, range(PARTS))
    low_lane = lax.broadcasted_iota(jnp.int32, (spots, LANES), 1) < LANES // 2
    for b in range(2):
        for d in range(2):
            @pl.when(exists(d, last + 1))
            def _(d=d, b=b):
                @pl.loop(0, 2)
                def _(core):
                    project_tile(2 * source(d, last + 1) + core, b)

        part = lacc[pl.ds(b * tile, tile)]
        folded = part + pltpu.roll(part, LANES // 2, 1)
        lpo[b] = jnp.where(low_lane, folded[:spots], folded[spots:])
        low_copy(b).start()
        if b == 0:
            for q in (ups_part, scale_part):
                z_events(last, q)
    for k in range(depth - 1):
        y_events(k, ups_part)
    for c in range(2):
        part_copy(c).wait_recv()
    for copy in own_copies(1 - s)[1:]:
        copy.wait_recv()
    for k in range(depth - 1):
        for d in range(2):
            arrived(d, k, (ups_part, scale_part))

    end_tile = min(256, spots)
    for b in range(2):
        low_copy(b).wait_recv()
        both = lpo[b] + lpi[b]
        turned = pltpu.roll(both, LANES // 2, 1)
        lacc[pl.ds(b * tile, spots)] = jnp.where(low_lane, both, turned)
        lacc[pl.ds(b * tile + spots, spots)] = jnp.where(low_lane, turned, both)

        @pl.loop(0, tile // end_tile)
        def _(i, b=b):
            at = pl.ds(pl.multiple_of(b * tile + i * end_tile, end_tile), end_tile)
            low = lacc[at].astype(jnp.bfloat16).astype(jnp.float32)
            key = key_ref[at]
            scale = jnp.zeros_like(low)
            spread = []
            for j in range(4 * depth):
                mine = key == 2 * j
                scale += jnp.where(mine, scales[j // 2, pl.ds(j % 2, 1)], 0.0)
                spread.append(jnp.where(mine, low, 0.0).astype(jnp.bfloat16))
            spread = jnp.concatenate(spread, axis=1)
            scale += pltpu.roll(scale, LANES // 2, 1)
            for c in range(2):
                cols = pl.ds(c * half_outs, half_outs)
                delta = jnp.dot(
                    spread, ups[:, :, cols].reshape(-1, half_outs), preferred_element_type=jnp.float32
                )
                wide_scale = jnp.concatenate([scale] * (half_outs // LANES), axis=1)
                delta = (delta * wide_scale).astype(jnp.bfloat16).astype(jnp.float32)
                base = acc[at, cols] + pin[c, at].astype(jnp.float32)
                out_ref[at, cols] = (base + delta).astype(jnp.bfloat16)

    for c in range(2):
        x_copy(c).wait_send()
        xc_copy(c, s).wait_send()
        part_copy(c).wait_send()
    for b in range(2):
        low_copy(b).wait_send()
    for copy in own_copies(s):
        copy.wait_send()
    for k in range(depth - 1):
        for d in range(2):
            @pl.when(exists(d, k) & can_send(d))
            def _(d=d, k=k):
                for q in range(PARTS + 2):
                    z_copy(d, k, q).wait_send()

            @pl.when(exists(d, k + 1))
            def _(d=d, k=k):
                for q in range(PARTS + 2):
                    c_copy(d, k, q, 0, s).wait_send()
                    if q != scale_part:
                        y_copy(d, k, q, g).wait_send()
                        c_copy(d, k, q, 1, s).wait_send()


def fused(depth, tokens, named, table, base, down_rows, up_rows, scale_rows):
    rows, feats = tokens.shape
    held_rows, outs = up_rows.shape
    bf16, f32 = jnp.bfloat16, jnp.float32
    hops = (2, depth - 1, PARTS + 2)
    any_spec = pl.BlockSpec(memory_space=pl.ANY)
    vmem = pl.BlockSpec(memory_space=pltpu.VMEM)
    smem = pl.BlockSpec(memory_space=pltpu.SMEM)
    return pl.pallas_call(
        functools.partial(kernel, depth),
        out_shape=jax.ShapeDtypeStruct((rows, outs), bf16),
        in_specs=[any_spec] * 4 + [vmem, smem, smem],
        out_specs=vmem,
        scratch_shapes=[
            pltpu.VMEM((rows, feats), bf16),
            pltpu.VMEM((feats, outs), bf16),
            pltpu.VMEM((2, feats, outs // 2), bf16),
            pltpu.VMEM((2 * depth, held_rows, feats), bf16),
            pltpu.VMEM((2 * depth, held_rows, outs), bf16),
            pltpu.VMEM((2 * depth, 8, LANES), f32),
            pltpu.VMEM((rows, LANES), jnp.int32),
            pltpu.VMEM((rows, outs), f32),
            pltpu.VMEM((2, rows, outs // 2), bf16),
            pltpu.VMEM((2, rows, outs // 2), bf16),
            pltpu.VMEM((rows, LANES), f32),
            pltpu.VMEM((2, rows // 4, LANES), f32),
            pltpu.VMEM((2, rows // 4, LANES), f32),
            pltpu.SemaphoreType.DMA((4,)),
            pltpu.SemaphoreType.DMA(hops),
            pltpu.SemaphoreType.DMA(hops),
            pltpu.SemaphoreType.DMA(hops),
            pltpu.SemaphoreType.DMA(hops),
            pltpu.SemaphoreType.DMA(hops + (2,)),
            pltpu.SemaphoreType.DMA(hops + (2,)),
            pltpu.SemaphoreType.DMA((11,)),
            pltpu.SemaphoreType.DMA((11,)),
        ],
        compiler_params=pltpu.CompilerParams(
            collective_id=0, has_side_effects=True, vmem_limit_bytes=58 * 1024 * 1024
        ),
    )(tokens, base, down_rows, up_rows, named.reshape(rows // LANES, LANES), table, scale_rows)


def plain(tokens, stored, base, down_rows, up_rows, scale_rows, adapters):
    rows = tokens.shape[0]
    rank = down_rows.shape[0] // scale_rows.shape[0]
    owners = ("adapters", "sub")
    down_all = lax.all_gather(down_rows, owners, axis=0, tiled=True)
    up_all = lax.all_gather(up_rows, owners, axis=0, tiled=True)
    scale_all = lax.all_gather(scale_rows, owners, axis=0, tiled=True)
    base_rows = lax.all_to_all(base, "tp", split_axis=0, concat_axis=1, tiled=True)
    base_sum = lax.psum_scatter(
        jnp.dot(tokens, base_rows, preferred_element_type=jnp.float32),
        "tp", scatter_dimension=1, tiled=True,
    )
    one_hot = stored[:, None] == jnp.arange(adapters, dtype=jnp.int32)[None, :]
    wide = lax.dot_general(
        tokens, down_all, (((1,), (1,)), ((), ())), preferred_element_type=jnp.float32
    )
    low = jnp.sum(jnp.where(one_hot[:, :, None], wide.reshape(rows, adapters, rank), 0.0), axis=1)
    low = lax.psum(low, "tp").astype(jnp.bfloat16)
    spread = jnp.where(one_hot[:, :, None], low[:, None, :], 0).reshape(rows, adapters * rank)
    delta = jnp.dot(spread, up_all, preferred_element_type=jnp.float32)
    scale = jnp.sum(jnp.where(one_hot, scale_all[None, :], 0.0), axis=1)
    delta = (delta * scale[:, None]).astype(jnp.bfloat16)
    return (base_sum + delta.astype(jnp.float32)).astype(jnp.bfloat16)


def local(
    sizes, tokens, token_adapter_index, adapter_slot_table, base, down, up, scale_rows
):
    held, feats, rank = down.shape
    adapters = adapter_slot_table.shape[0]
    outs = base.shape[1]
    down_rows = jnp.swapaxes(down, 1, 2).reshape(held * rank, feats)
    up_rows = up.reshape(held * rank, outs)
    depth = sizes["adapters"]
    small = sizes["groups"] == sizes["tp"] == sizes["sub"] == 2 and 2 <= depth <= 4
    if small and held == 4 and 2 * rank == LANES:
        return fused(
            depth, tokens, token_adapter_index, adapter_slot_table, base, down_rows, up_rows, scale_rows
        )
    slots = jnp.arange(adapters, dtype=jnp.int32)
    named = token_adapter_index == slots[None, :]
    stored = jnp.sum(jnp.where(named, adapter_slot_table[None, :], 0), axis=1)
    return plain(tokens, stored, base, down_rows, up_rows, scale_rows, adapters)


def solution(mesh):
    in_specs = (
        P(("groups", "adapters", "sub"), "tp"),
        P(("groups", "adapters", "sub"), None),
        P(),
        P(None, "tp"),
        P(("adapters", "sub"), "tp", None),
        P(("adapters", "sub"), None, "tp"),
        P(("adapters", "sub")),
    )
    out_specs = P(("groups", "adapters", "sub"), "tp")
    return jax.shard_map(
        functools.partial(local, dict(mesh.shape)), mesh=mesh,
        in_specs=in_specs, out_specs=out_specs, check_vma=False,
    )
```

time: 128 us -> 115 us (0.90)
  Pallas kernels: 121 us -> 113 us
  other arithmetic: 4.26 us -> 0 us
    pallas_call x1, Pallas kernels: 121 us -> 113 us  [fused(): pl.pallas_call(functools.partial(kernel, depth), out_shape=jax.ShapeDtype...]
    concatenate x1 -> x0, other arithmetic: 1.72 us -> none  [fused(): up_wide = jnp.concatenate([up_rows, scale_cols], axis=1)]
where the time goes in v2:
time: 115 us
  Pallas kernels  113 us (98%)
  local copies, waits for them, and re-layouts  2.26 us (2%)
    pallas_call x1, Pallas kernels, fused(): pl.pallas_call(functools.partial(kernel, depth), out_shape=jax.ShapeDtype...  113 us

profile of v2, /device:TPU:0, one launch (start us, length us, event | category | flops | bytes accessed | tf_op | source)
XLA Modules:
  0.0 115.3 jit_solution(4482491438654394793)
XLA Ops:
  0.0 113.0 %shard_map.73 = bf16[1024,512]{1,0:T(8,128)(2,1)} custom-call(bf16[1024,4096]{1,0:T(8,128)(2,1)} %tok_hbm.1, bf16[8192,512]{1,0:T(8,128)(2,1)} %base_hbm.1, bf16[256,4096]{1,0:T(8,128)(2,1)} %bitcast.5, bf16[256,512]{1,0:T(8,128)(2,1)} %bitcast.6, s32[8,128]{1,0:T(8,128)} %bitcast.7, s32[32]{0:T(128)} %table_ref.1, f32[4]{0:T(128)} %scale_ref.1), custom_call_target="tpu_custom_call" | custom-call | tf_op jit(solution)/shard_map/pallas_call | solution.py:351
  113.0 2.3 %copy.9 = bf16[1024,512]{1,0:T(8,128)(2,1)} copy(bf16[1024,512]{1,0:T(8,128)(2,1)} %shard_map.73) | data formatting | bytes 2097152
